TPU v7x, 1024 devices: a whole 4x4x32 slice. The times are simulated.
1024 devices in a mesh: node: 128 (over z, x), local: 8 (over y, core).
Axes of the slice: x: 4, y: 4, z: 32, core: 2. Of those that a mesh axis runs over, the one named last changes fastest.
Arguments:
- tokens: bfloat16 [1024, 7168], P('node', 'local'), may hold values from -6 to 6
- cotangent: bfloat16 [1024, 7168], P('node', 'local'), may hold values from -6 to 6
- routes: int32 [1024, 2], P('node'), may hold values from 0 to 15, all different within a row; in each aligned block of 8 rows (0 to 7, 8 to 15, ...) at most 2 rows name the same one
- gates: float32 [1024, 2], P('node'), may hold values from 0.2 to 1
- w_gate: bfloat16 [7168, 32768], P('local', 'node'), may hold values from -0.0625 to 0.0625
- w_up: bfloat16 [7168, 32768], P('local', 'node'), may hold values from -0.0625 to 0.0625
- w_down: bfloat16 [32768, 7168], P('node', 'local'), may hold values from -0.125 to 0.125
Outputs:
- mixed: bfloat16 [1024, 7168], P('node', 'local')
- d_tokens: bfloat16 [1024, 7168], P('node', 'local')
- d_gate: bfloat16 [7168, 32768], P('local', 'node')
- d_up: bfloat16 [7168, 32768], P('local', 'node')
- d_down: bfloat16 [32768, 7168], P('node', 'local')
Inputs may be any that keep to these rules, and one draw needn't show every extreme that they name: `routes`: each row names 2 different experts; the pairs of one block of 8 rows name one expert at most 2 times, a bound that some block reaches.
All inputs are finite; a program needn't handle non-finite values.
Results may differ from a plain program's by a relative error of at most 0.02.
Values may be sent and summed in bfloat16 or wider, within the bound.
A program may use at most 32 MiB of HBM per device.

v0:
```python
import jax
import jax.numpy as jnp
from jax import lax
from jax.sharding import PartitionSpec as P

TOP = 2


def slot_tables(routes, gates, experts_all, capacity):
    tok_rows = routes.shape[0]
    flat = routes.reshape(tok_rows * TOP)
    experts = jnp.arange(experts_all, dtype=jnp.int32)
    hot = (flat[:, None] == experts[None, :]).astype(jnp.int32)
    before = jnp.cumsum(hot, axis=0) - hot
    slot = jnp.sum(before * hot, axis=1)
    slots = jnp.arange(capacity, dtype=jnp.int32)
    picks = (
        (flat[None, None, :] == experts[:, None, None])
        & (slot[None, None, :] == slots[None, :, None])
    ).astype(jnp.float32)
    picks = picks.reshape(experts_all, capacity, tok_rows, TOP)
    member = jnp.sum(picks, axis=3)
    weighted = jnp.sum(picks * gates.reshape(1, 1, tok_rows, TOP), axis=3)
    return (member, weighted)


def local(tokens, cotangent, routes, gates, w_gate, w_up, w_down):
    shares = max(1, lax.axis_size("node") // 16)
    experts_all = lax.axis_size("node") // shares
    tok_rows = tokens.shape[0]
    capacity = min(tok_rows, tok_rows * TOP * 2 // experts_all)
    member, weighted = slot_tables(routes, gates, experts_all, capacity)
    slot_x = jnp.einsum("ect,td->ecd", member, tokens.astype(jnp.float32)).astype(jnp.bfloat16)
    slot_g = jnp.einsum("ect,td->ecd", weighted, cotangent.astype(jnp.float32)).astype(jnp.bfloat16)
    send_x = jnp.repeat(slot_x, shares, axis=0)
    send_g = jnp.repeat(slot_g, shares, axis=0)
    width = tokens.shape[1]
    recv_x = lax.all_to_all(send_x, "node", split_axis=0, concat_axis=0, tiled=True)
    rows_x = recv_x.reshape(-1, width)
    a_part = jnp.dot(rows_x, w_gate, preferred_element_type=jnp.float32)
    b_part = jnp.dot(rows_x, w_up, preferred_element_type=jnp.float32)
    a_val, b_val = lax.psum((a_part, b_part), "local")
    sig = jax.nn.sigmoid(a_val)
    hidden = (a_val * sig * b_val).astype(jnp.bfloat16)
    out_part = jnp.dot(hidden, w_down, preferred_element_type=jnp.float32).astype(jnp.bfloat16)
    recv_g = lax.all_to_all(send_g, "node", split_axis=0, concat_axis=0, tiled=True)
    rows_g = recv_g.reshape(-1, width)
    dh_part = jnp.dot(rows_g, w_down.T, preferred_element_type=jnp.float32)
    dh_val = lax.psum(dh_part, "local")
    d_down = jnp.dot(hidden.T, rows_g, preferred_element_type=jnp.float32).astype(jnp.bfloat16)
    grad_a = (dh_val * b_val * sig * (1.0 + a_val * (1.0 - sig))).astype(jnp.bfloat16)
    grad_b = (dh_val * a_val * sig).astype(jnp.bfloat16)
    d_gate = jnp.dot(rows_x.T, grad_a, preferred_element_type=jnp.float32).astype(jnp.bfloat16)
    d_up = jnp.dot(rows_x.T, grad_b, preferred_element_type=jnp.float32).astype(jnp.bfloat16)
    dx_part = (
        jnp.dot(grad_a, w_gate.T, preferred_element_type=jnp.float32)
        + jnp.dot(grad_b, w_up.T, preferred_element_type=jnp.float32)
    ).astype(jnp.bfloat16)
    out_back, dx_back = (
        lax.all_to_all(
            out_part.reshape(send_x.shape), "node", split_axis=0, concat_axis=0, tiled=True
        ),
        lax.all_to_all(
            dx_part.reshape(send_x.shape), "node", split_axis=0, concat_axis=0, tiled=True
        ),
    )
    out_sum = jnp.sum(
        out_back.reshape(experts_all, shares, capacity, width).astype(jnp.float32), axis=1
    )
    dx_sum = jnp.sum(
        dx_back.reshape(experts_all, shares, capacity, width).astype(jnp.float32), axis=1
    )
    mixed = jnp.einsum("ect,ecd->td", weighted, out_sum).astype(jnp.bfloat16)
    d_tokens = jnp.einsum("ect,ecd->td", member, dx_sum).astype(jnp.bfloat16)
    return (mixed, d_tokens, d_gate, d_up, d_down)


def solution(mesh):
    placed = (
        P("node", "local"),
        P("node", "local"),
        P("node", None),
        P("node", None),
        P("local", "node"),
        P("local", "node"),
        P("node", "local"),
    )
    return jax.shard_map(
        local,
        mesh=mesh,
        in_specs=placed,
        out_specs=(
            P("node", "local"),
            P("node", "local"),
            P("local", "node"),
            P("local", "node"),
            P("node", "local"),
        ),
        check_vma=False,
    )
```

profile of v0, /device:TPU:6, one launch (start us, length us, event | category | flops | bytes accessed | tf_op | source)
XLA Modules:
  0.0 407.0 jit_solution(3368691985960121509)
XLA Ops:
  7.2 0.0 copy-start
  7.2 0.0 copy-start.5
  7.2 0.8 copy.29
  8.0 0.0 copy-done.5
  8.0 0.1 iota_compare_fusion.1
  8.1 0.1 eq.56
  8.2 0.1 fusion.9
  8.3 0.0 copy-start.6
  8.3 0.2 select_reduce_fusion
  8.5 0.0 copy-start.3
  8.5 0.1 eq.60
  8.6 0.1 copy.30
  8.6 0.3 copy-done.6
  9.0 0.1 fusion.6
  9.0 0.1 copy-done.3
  9.2 0.2 convolution_convert_fusion.5
  9.4 1.0 broadcast_in_dim.4
  10.4 0.0 copy-start.4
  10.5 32.7 %all-to-all-start = ((bf16[128,2,896]{2,1,0:T(2,128)(2,1)}), bf16[128,2,896]{2,1,0:T(2,128)(2,1)S(1)}, u32[]{:S(2)}, u32[]{:S(2)}) async-start(bf16[128,2,896]{2,1,0:T(2,128)(2,1)} %bitcast.1), calls=%async_computation | async-start | bytes 917504 | tf_op jit(solution)/shard_map/all_to_all | solution.py:38
  43.2 0.0 copy-done.4
  43.2 0.2 convolution_convert_fusion.4
  43.5 57.8 %all-to-all-done = bf16[128,2,896]{2,1,0:T(2,128)(2,1)S(1)} async-done(((bf16[128,2,896]{2,1,0:T(2,128)(2,1)}), bf16[128,2,896]{2,1,0:T(2,128)(2,1)S(1)}, u32[]{:S(2)}, u32[]{:S(2)}) %all-to-all-start) | async-done | bytes 458784 | tf_op jit(solution)/shard_map/all_to_all | solution.py:38
  101.2 1.0 broadcast_in_dim.5
  102.3 7.6 %all-to-all-start.2 = ((bf16[128,2,896]{2,1,0:T(2,128)(2,1)}), bf16[128,2,896]{2,1,0:T(2,128)(2,1)S(1)}, u32[]{:S(2)}, u32[]{:S(2)}) async-start(bf16[128,2,896]{2,1,0:T(2,128)(2,1)} %bitcast.5), calls=%async_computation.2 | async-start | bytes 917504 | tf_op jit(solution)/shard_map/all_to_all | solution.py:46
  109.9 0.0 all-reduce.3.cloned.1.call-start
  109.9 0.2 reshape.94
  110.1 0.0 copy-done
  110.1 0.0 copy-start.2
  110.1 1.0 fusion.10
  111.1 0.0 copy-done.2
  111.1 1.0 fusion.11
  112.1 0.0 copy-start.1
  112.1 55.2 %all-to-all-done.2 = bf16[128,2,896]{2,1,0:T(2,128)(2,1)S(1)} async-done(((bf16[128,2,896]{2,1,0:T(2,128)(2,1)}), bf16[128,2,896]{2,1,0:T(2,128)(2,1)S(1)}, u32[]{:S(2)}, u32[]{:S(2)}) %all-to-all-start.2) | async-done | bytes 458784 | tf_op jit(solution)/shard_map/all_to_all | solution.py:46
  167.3 0.2 reshape.97
  167.5 0.0 copy-done.1
  167.5 1.0 fusion.12
  168.5 0.0 all-reduce.3.cloned.1.call-update
  168.5 80.4 %all-reduce.3.cloned.1.call-done = (f32[256,256]{1,0:T(8,128)}, f32[256,256]{1,0:T(8,128)}, f32[256,256]{1,0:T(8,128)}) async-done(((f32[256,256]{1,0:T(8,128)}, f32[256,256]{1,0:T(8,128)}, f32[256,256]{1,0:T(8,128)}), (f32[256,256]{1,0:T(8,128)}, f32[256,256]{1,0:T(8,128)}, f32[256,256]{1,0:T(8,128)})) %all-reduce.3.cloned.1.call-update) | async-done | bytes 786448 | tf_op jit(solution)/shard_map/psum | solution.py:42
  248.9 1.2 multiply_convert_fusion
  250.2 0.3 fusion.13
  250.5 0.3 fusion
  250.8 0.9 reshape.98
  251.8 26.8 %all-to-all-start.3 = ((bf16[128,2,896]{2,1,0:T(2,128)(2,1)}), bf16[128,2,896]{2,1,0:T(2,128)(2,1)S(1)}, u32[]{:S(2)}, u32[]{:S(2)}) async-start(bf16[128,2,896]{2,1,0:T(2,128)(2,1)} %reshape.98), calls=%async_computation.3 | async-start | bytes 917504 | tf_op jit(solution)/shard_map/all_to_all | solution.py:63
  278.6 0.3 convolution_convert_fusion.3
  278.9 0.9 reshape.95
  279.8 54.8 %all-to-all-done.3 = bf16[128,2,896]{2,1,0:T(2,128)(2,1)S(1)} async-done(((bf16[128,2,896]{2,1,0:T(2,128)(2,1)}), bf16[128,2,896]{2,1,0:T(2,128)(2,1)S(1)}, u32[]{:S(2)}, u32[]{:S(2)}) %all-to-all-start.3) | async-done | bytes 458784 | tf_op jit(solution)/shard_map/all_to_all | solution.py:63
  334.7 7.7 %all-to-all-start.1 = ((bf16[128,2,896]{2,1,0:T(2,128)(2,1)}), bf16[128,2,896]{2,1,0:T(2,128)(2,1)S(1)}, u32[]{:S(2)}, u32[]{:S(2)}) async-start(bf16[128,2,896]{2,1,0:T(2,128)(2,1)} %reshape.95), calls=%async_computation.1 | async-start | bytes 917504 | tf_op jit(solution)/shard_map/all_to_all | solution.py:60
  342.3 1.1 convolution_convert_fusion
  343.4 1.1 convolution_convert_fusion.1
  344.5 1.1 convolution_convert_fusion.2
  345.6 0.4 convert_reduce_fusion
  346.0 0.8 fusion.2
  346.8 52.2 %all-to-all-done.1 = bf16[128,2,896]{2,1,0:T(2,128)(2,1)S(1)} async-done(((bf16[128,2,896]{2,1,0:T(2,128)(2,1)}), bf16[128,2,896]{2,1,0:T(2,128)(2,1)S(1)}, u32[]{:S(2)}, u32[]{:S(2)}) %all-to-all-start.1) | async-done | bytes 458784 | tf_op jit(solution)/shard_map/all_to_all | solution.py:60
  399.0 0.4 convert_reduce_fusion.1
  399.4 0.8 fusion.1
  (4 shorter events, 0.1 us)
Async XLA Ops:
  7.2 102.9 %copy-start = (bf16[896,256]{1,0:T(8,128)(2,1)S(1)}, bf16[896,256]{1,0:T(8,128)(2,1)}, u32[]{:S(2)}) copy-start(bf16[896,256]{1,0:T(8,128)(2,1)} %param.11) | copy-start | bytes 1376260
  7.2 0.8 copy-start.5
  8.3 0.7 copy-start.6
  8.5 0.7 copy-start.3
  10.4 32.8 %copy-start.4 = (bf16[8,896]{1,0:T(8,128)(2,1)S(1)}, bf16[8,896]{1,0:T(8,128)(2,1)}, u32[]{:S(2)}) copy-start(bf16[8,896]{1,0:T(8,128)(2,1)} %param.8) | copy-start | bytes 43012
  10.5 90.8 %all-to-all-start = ((bf16[128,2,896]{2,1,0:T(2,128)(2,1)}), bf16[128,2,896]{2,1,0:T(2,128)(2,1)S(1)}, u32[]{:S(2)}, u32[]{:S(2)}) async-start(bf16[128,2,896]{2,1,0:T(2,128)(2,1)} %bitcast.1), calls=%async_computation | async-start | bytes 917504 | tf_op jit(solution)/shard_map/all_to_all | solution.py:38
  102.3 65.0 %all-to-all-start.2 = ((bf16[128,2,896]{2,1,0:T(2,128)(2,1)}), bf16[128,2,896]{2,1,0:T(2,128)(2,1)S(1)}, u32[]{:S(2)}, u32[]{:S(2)}) async-start(bf16[128,2,896]{2,1,0:T(2,128)(2,1)} %bitcast.5), calls=%async_computation.2 | async-start | bytes 917504 | tf_op jit(solution)/shard_map/all_to_all | solution.py:46
  109.9 139.1 %all-reduce.3.cloned.1.call-start = ((), (), s32[]{:S(2)}) async-start(), calls=%async_computation.4 | async-start | bytes 1572864 | tf_op jit(solution)/shard_map/psum | solution.py:42
  110.1 1.0 copy-start.2
  112.1 55.3 %copy-start.1 = (bf16[256,896]{1,0:T(8,128)(2,1)S(1)}, bf16[256,896]{1,0:T(8,128)(2,1)}, u32[]{:S(2)}) copy-start(bf16[256,896]{1,0:T(8,128)(2,1)} %param.13) | copy-start | bytes 1376260
  251.8 82.9 %all-to-all-start.3 = ((bf16[128,2,896]{2,1,0:T(2,128)(2,1)}), bf16[128,2,896]{2,1,0:T(2,128)(2,1)S(1)}, u32[]{:S(2)}, u32[]{:S(2)}) async-start(bf16[128,2,896]{2,1,0:T(2,128)(2,1)} %reshape.98), calls=%async_computation.3 | async-start | bytes 917504 | tf_op jit(solution)/shard_map/all_to_all | solution.py:63
  334.7 64.3 %all-to-all-start.1 = ((bf16[128,2,896]{2,1,0:T(2,128)(2,1)}), bf16[128,2,896]{2,1,0:T(2,128)(2,1)S(1)}, u32[]{:S(2)}, u32[]{:S(2)}) async-start(bf16[128,2,896]{2,1,0:T(2,128)(2,1)} %reshape.95), calls=%async_computation.1 | async-start | bytes 917504 | tf_op jit(solution)/shard_map/all_to_all | solution.py:60
Sparse Core Ops, SparseCore 0:
  168.7 80.1 all-reduce.2
where the time goes:
time: 409 us; the launch traced here: 407 us
  waiting for transfers between devices  300 us (73%)
  starting transfers between devices  74.9 us (18%)
  between operations  14.2 us (3%)
  matrix products  9.28 us (2%)
  local copies, waits for them, and re-layouts  5.88 us (1%)
    psum x1, waiting for transfers between devices, local(): a_val, b_val = lax.psum((a_part, b_part), 'local')  80.4 us
    all_to_all x1, waiting for transfers between devices, local(): lax.all_to_all(send_x, 'node', split_axis=0, concat_axis=0, tiled=True)  57.8 us
    all_to_all x1, waiting for transfers between devices, local(): lax.all_to_all(send_g, 'node', split_axis=0, concat_axis=0, tiled=True)  55.2 us
    all_to_all x1, waiting for transfers between devices, local(): lax.all_to_all(dx_part.reshape(send_x.shape), 'node', split_axis=0, conca...  54.8 us
    all_to_all x1, waiting for transfers between devices, local(): lax.all_to_all(out_part.reshape(send_x.shape), 'node', split_axis=0, conc...  52.2 us
    all_to_all x1, starting transfers between devices, local(): lax.all_to_all(send_x, 'node', split_axis=0, concat_axis=0, tiled=True)  32.7 us
    all_to_all x1, starting transfers between devices, local(): lax.all_to_all(dx_part.reshape(send_x.shape), 'node', split_axis=0, conca...  26.8 us
  transfers between devices with their start and end apart: 5, of which 5 were waited for; matrix products, arithmetic and copies ran while one was open for 2% of the time, Pallas kernels for 0%

commit v1 on v0

v1 whole, which is shorter than its diff:
```python
import functools

import jax
import jax.numpy as jnp
from jax import lax
from jax.experimental import pallas as pl
from jax.experimental.pallas import tpu as pltpu
from jax.sharding import PartitionSpec as P

MESH = pl.DeviceIdType.MESH
BF = jnp.bfloat16
F32 = jnp.float32
I32 = jnp.int32
EXPERTS = 16
UNIT = 16

(DX, DG, GX, GG, SAB, SDH, AH, AD, RO, RX, BO, BX) = range(12)


def iotas(shape):
    return lax.broadcasted_iota(I32, shape, 0), lax.broadcasted_iota(I32, shape, 1)


def pick_table(rows, cols, routes, gates):
    expert, token = rows >> 4, cols & 7
    hot = jnp.zeros(rows.shape, F32)
    before = jnp.zeros(rows.shape, F32)
    gate = jnp.zeros(rows.shape, F32)
    for t in range(8):
        first, second = expert == routes[0, t], expert == routes[1, t]
        here = token == t
        named = jnp.where(first | second, 1.0, 0.0)
        hot = hot + jnp.where(here, named, 0.0)
        before = before + jnp.where(token > t, named, 0.0)
        weight = jnp.where(first, gates[0, t], 0.0) + jnp.where(second, gates[1, t], 0.0)
        gate = gate + jnp.where(here, weight, 0.0)
    slot = (rows & 1).astype(F32)
    keep = (((rows & 15) >> 1) == (cols >> 3)) & (before == slot)
    return jnp.where(keep, hot, 0.0), jnp.where(keep, gate, 0.0)


def stacked(value, chunks):
    parts = [value[:, j * 128 : (j + 1) * 128] for j in range(chunks)]
    parts = parts + [jnp.zeros_like(parts[0])] * (8 - chunks)
    return jnp.concatenate(parts, axis=0)


def kernel(
    sizes,
    tokens, cot, routes, gates, w_gate, w_up, w_down,
    mixed, d_tokens, d_gate, d_up, d_down,
    slot_x, slot_g, got_x, got_g, all_x, all_g, w_in, w_out,
    part_ab, sum_ab, part_dh, sum_dh, hid, grads,
    out_s, out_r, dx_s, dx_r, back_os, back_or, back_xs, back_xr,
    grad_in, grad_out, spread,
    send, recv, loads,
):
    ne, ns, nl = sizes
    width = tokens.shape[1]
    chunks = width // 128
    hidden_n = w_gate.shape[1]
    per = ne * 2
    rows_all = per * ns
    piece = rows_all // nl
    node, loc = lax.axis_index("node"), lax.axis_index("local")
    expert, shard = node // ns, node % ns

    fetch = [
        pltpu.make_async_copy(w_gate, w_in.at[:, pl.ds(0, hidden_n)], loads.at[0]),
        pltpu.make_async_copy(w_up, w_in.at[:, pl.ds(hidden_n, hidden_n)], loads.at[1]),
        pltpu.make_async_copy(w_down, w_out, loads.at[2]),
    ]
    for copy in fetch:
        copy.start()

    far = sorted(range(1, ne), key=lambda d: -min(d, ne - d))
    by_expert = [(lax.rem(expert + d, ne) * ns + shard, loc, lax.rem(expert + d, ne)) for d in far]
    by_shard = []
    for d in range(1, ns):
        other = lax.rem(shard + d, ns)
        by_shard.append((expert * ns + other, loc, other))
    by_local = []
    for d in range(1, nl):
        other = lax.rem(loc + d, nl)
        by_local.append((node, other, other))

    barrier = pltpu.get_barrier_semaphore()
    everyone = by_expert + by_shard + by_local
    for to_node, to_loc, _ in everyone:
        pl.semaphore_signal(
            barrier, inc=1, device_id={"node": to_node, "local": to_loc}, device_id_type=MESH
        )

    def push(phase, peers, source, target):
        for to_node, to_loc, index in peers:
            pltpu.make_async_remote_copy(
                src_ref=source(index),
                dst_ref=target(index),
                send_sem=send.at[phase],
                recv_sem=recv.at[phase],
                device_id={"node": to_node, "local": to_loc},
                device_id_type=MESH,
            ).start()

    def arrived(phase, ref, count):
        if count:
            part = ref.at[pl.ds(0, count)]
            pltpu.make_async_copy(part, part, recv.at[phase]).wait()

    def sent(phase, ref, count):
        if count:
            part = ref.at[pl.ds(0, count)]
            pltpu.make_async_copy(part, part, send.at[phase]).wait()

    def rows(ref, index, n):
        return ref.at[pl.ds(pl.multiple_of(index * n, n), n)]

    unit_rows = ne * UNIT
    member, weighted = pick_table(*iotas((unit_rows, 64)), routes, gates)
    pick = member.astype(BF)
    slot_gate = jnp.sum(weighted, axis=1, keepdims=True)
    tok = stacked(tokens[...].astype(F32), chunks).astype(BF)
    slot_x[...] = jnp.dot(pick, tok, preferred_element_type=F32).astype(BF)
    grad_rows = stacked(cot[...].astype(F32), chunks).astype(BF)
    slot_g[...] = (jnp.dot(pick, grad_rows, preferred_element_type=F32) * slot_gate).astype(BF)

    pl.semaphore_wait(barrier, len(everyone))
    push(DX, by_expert, lambda e: rows(slot_x, e, UNIT), lambda e: rows(got_x, expert, UNIT))
    push(DG, by_expert, lambda e: rows(slot_g, e, UNIT), lambda e: rows(got_g, expert, UNIT))
    own_unit = pl.ds(pl.multiple_of(expert * UNIT, UNIT), UNIT)
    got_x[own_unit, :] = slot_x[own_unit, :]
    got_g[own_unit, :] = slot_g[own_unit, :]

    a, b = iotas((chunks * per, unit_rows))
    q = lax.rem(a, per)
    spread[...] = jnp.where(b == (q >> 1) * UNIT + 2 * (a // per) + (q & 1), 1.0, 0.0).astype(BF)

    own_rows = pl.ds(pl.multiple_of(shard * per, per), per)

    def unfold(ref, target):
        flat = jnp.dot(spread[...], ref[...], preferred_element_type=F32).astype(BF)
        for j in range(chunks):
            target[own_rows, j * 128 : (j + 1) * 128] = flat[j * per : (j + 1) * per, :]

    arrived(DX, got_x, (ne - 1) * UNIT)
    unfold(got_x, all_x)
    push(GX, by_shard, lambda s: all_x.at[own_rows], lambda s: all_x.at[own_rows])
    arrived(DG, got_g, (ne - 1) * UNIT)
    unfold(got_g, all_g)
    push(GG, by_shard, lambda s: all_g.at[own_rows], lambda s: all_g.at[own_rows])

    for copy in fetch:
        copy.wait()
    arrived(GX, all_x, (ns - 1) * per)
    part_ab[...] = jnp.dot(all_x[...], w_in[...], preferred_element_type=F32).astype(BF)
    push(SAB, by_local, lambda l: rows(part_ab, l, piece), lambda l: rows(sum_ab, loc, piece))
    mine = pl.ds(pl.multiple_of(loc * piece, piece), piece)
    sum_ab[mine, :] = part_ab[mine, :]

    arrived(GG, all_g, (ns - 1) * per)
    part_dh[...] = lax.dot_general(
        all_g[...], w_out[...], (((1,), (1,)), ((), ())), preferred_element_type=F32
    ).astype(BF)
    push(SDH, by_local, lambda l: rows(part_dh, l, piece), lambda l: rows(sum_dh, loc, piece))
    sum_dh[mine, :] = part_dh[mine, :]

    def total(ref, n, count):
        value = ref[0:n, :].astype(F32)
        for i in range(1, count):
            value = value + ref[i * n : (i + 1) * n, :].astype(F32)
        return value

    arrived(SAB, sum_ab, (nl - 1) * piece)
    ab = total(sum_ab, piece, nl)
    a_val, b_val = ab[:, :hidden_n], ab[:, hidden_n:]
    sig = jax.nn.sigmoid(a_val)
    hid[mine, :] = (a_val * sig * b_val).astype(BF)
    push(AH, by_local, lambda l: hid.at[mine], lambda l: hid.at[mine])

    arrived(SDH, sum_dh, (nl - 1) * piece)
    dh = total(sum_dh, piece, nl)
    grads[mine, 0:hidden_n] = (dh * b_val * sig * (1.0 + a_val * (1.0 - sig))).astype(BF)
    grads[mine, hidden_n : 2 * hidden_n] = (dh * a_val * sig).astype(BF)
    push(AD, by_local, lambda l: grads.at[mine], lambda l: grads.at[mine])

    arrived(AH, hid, (nl - 1) * piece)
    out_s[...] = jnp.dot(hid[...], w_out[...], preferred_element_type=F32).astype(BF)
    push(RO, by_shard, lambda s: rows(out_s, s, per), lambda s: rows(out_r, shard, per))
    out_r[own_rows, :] = out_s[own_rows, :]

    arrived(AD, grads, (nl - 1) * piece)
    dx_s[...] = lax.dot_general(
        grads[...], w_in[...], (((1,), (1,)), ((), ())), preferred_element_type=F32
    ).astype(BF)
    push(RX, by_shard, lambda s: rows(dx_s, s, per), lambda s: rows(dx_r, shard, per))
    dx_r[own_rows, :] = dx_s[own_rows, :]

    def fold(ref):
        value = total(ref, per, ns).astype(BF)
        tall = jnp.concatenate([value[:, j * 128 : (j + 1) * 128] for j in range(chunks)], axis=0)
        return lax.dot_general(
            spread[...], tall, (((0,), (0,)), ((), ())), preferred_element_type=F32
        ).astype(BF)

    arrived(RO, out_r, (ns - 1) * per)
    back_os[...] = fold(out_r)
    push(BO, by_expert, lambda e: rows(back_os, e, UNIT), lambda e: rows(back_or, expert, UNIT))
    back_or[own_unit, :] = back_os[own_unit, :]

    over_rows = (((0,), (0,)), ((), ()))
    grad_out[...] = lax.dot_general(
        hid[...], all_g[...], over_rows, preferred_element_type=F32
    ).astype(BF)
    grad_in[...] = lax.dot_general(
        all_x[...], grads[...], over_rows, preferred_element_type=F32
    ).astype(BF)
    store = [
        pltpu.make_async_copy(grad_in.at[:, pl.ds(0, hidden_n)], d_gate, loads.at[3]),
        pltpu.make_async_copy(grad_in.at[:, pl.ds(hidden_n, hidden_n)], d_up, loads.at[4]),
        pltpu.make_async_copy(grad_out, d_down, loads.at[5]),
    ]
    for copy in store:
        copy.start()

    arrived(RX, dx_r, (ns - 1) * per)
    back_xs[...] = fold(dx_r)
    push(BX, by_expert, lambda e: rows(back_xs, e, UNIT), lambda e: rows(back_xr, expert, UNIT))
    back_xr[own_unit, :] = back_xs[own_unit, :]

    cols, tall_rows = iotas((64, unit_rows))
    member_t, weighted_t = pick_table(tall_rows, cols, routes, gates)
    high = weighted_t.astype(BF)
    low = (weighted_t - high.astype(F32)).astype(BF)

    arrived(BO, back_or, (ne - 1) * UNIT)
    value = back_or[...]
    flat = jnp.dot(high, value, preferred_element_type=F32) + jnp.dot(
        low, value, preferred_element_type=F32
    )
    for j in range(chunks):
        mixed[:, j * 128 : (j + 1) * 128] = flat[j * 8 : (j + 1) * 8, :].astype(BF)
    arrived(BX, back_xr, (ne - 1) * UNIT)
    flat = jnp.dot(member_t.astype(BF), back_xr[...], preferred_element_type=F32)
    for j in range(chunks):
        d_tokens[:, j * 128 : (j + 1) * 128] = flat[j * 8 : (j + 1) * 8, :].astype(BF)

    sent(DX, slot_x, (ne - 1) * UNIT)
    sent(DG, slot_g, (ne - 1) * UNIT)
    sent(GX, all_x, (ns - 1) * per)
    sent(GG, all_g, (ns - 1) * per)
    sent(SAB, part_ab, (nl - 1) * piece)
    sent(SDH, part_dh, (nl - 1) * piece)
    sent(AH, hid, (nl - 1) * piece)
    sent(AD, grads, (nl - 1) * piece)
    sent(RO, out_s, (ns - 1) * per)
    sent(RX, dx_s, (ns - 1) * per)
    sent(BO, back_os, (ne - 1) * UNIT)
    sent(BX, back_xs, (ne - 1) * UNIT)
    for copy in store:
        copy.wait()


def local(sizes, tokens, cotangent, routes, gates, w_gate, w_up, w_down):
    ne, ns, nl = sizes
    toks, width = tokens.shape
    hidden_n = w_gate.shape[1]
    per = ne * 2
    rows_all = per * ns
    chunks = width // 128
    unit_rows = ne * UNIT
    vmem = pl.BlockSpec(memory_space=pltpu.VMEM)
    smem = pl.BlockSpec(memory_space=pltpu.SMEM)
    anywhere = pl.BlockSpec(memory_space=pl.ANY)
    unit = pltpu.VMEM((unit_rows, 128), BF)
    wide = pltpu.VMEM((rows_all, width), BF)
    scratch = (
        [unit] * 4
        + [wide] * 2
        + [pltpu.VMEM((width, 2 * hidden_n), BF), pltpu.VMEM((hidden_n, width), BF)]
        + [pltpu.VMEM((rows_all, 2 * hidden_n), BF)] * 2
        + [pltpu.VMEM((rows_all, hidden_n), BF)] * 2
        + [pltpu.VMEM((rows_all, hidden_n), BF), pltpu.VMEM((rows_all, 2 * hidden_n), BF)]
        + [wide] * 4
        + [unit] * 4
        + [pltpu.VMEM((width, 2 * hidden_n), BF), pltpu.VMEM((hidden_n, width), BF)]
        + [pltpu.VMEM((chunks * per, unit_rows), BF)]
        + [pltpu.SemaphoreType.DMA((12,)), pltpu.SemaphoreType.DMA((12,)), pltpu.SemaphoreType.DMA((6,))]
    )
    return pl.pallas_call(
        functools.partial(kernel, sizes),
        out_shape=(
            jax.ShapeDtypeStruct(tokens.shape, BF),
            jax.ShapeDtypeStruct(tokens.shape, BF),
            jax.ShapeDtypeStruct(w_gate.shape, BF),
            jax.ShapeDtypeStruct(w_up.shape, BF),
            jax.ShapeDtypeStruct(w_down.shape, BF),
        ),
        in_specs=[vmem, vmem, smem, smem, anywhere, anywhere, anywhere],
        out_specs=(vmem, vmem, anywhere, anywhere, anywhere),
        scratch_shapes=scratch,
        compiler_params=pltpu.CompilerParams(
            collective_id=0, has_side_effects=True, vmem_limit_bytes=32 * 1024 * 1024
        ),
        cost_estimate=pl.CostEstimate(flops=1_100_000_000, bytes_accessed=3_000_000, transcendentals=8192),
    )(tokens, cotangent, routes.T, gates.T, w_gate, w_up, w_down)


def build(mesh, experts):
    shards = mesh.shape["node"] // experts
    sizes = (experts, shards, mesh.shape["local"])
    return jax.shard_map(
        functools.partial(local, sizes),
        mesh=mesh,
        in_specs=(
            P("node", "local"),
            P("node", "local"),
            P("node", None),
            P("node", None),
            P("local", "node"),
            P("local", "node"),
            P("node", "local"),
        ),
        out_specs=(
            P("node", "local"),
            P("node", "local"),
            P("local", "node"),
            P("local", "node"),
            P("node", "local"),
        ),
        check_vma=False,
    )


def solution(mesh):
    return build(mesh, EXPERTS)
```

time: 409 us -> 104 us (0.25)
  the two profiles are of different devices: /device:TPU:6 before, /device:TPU:38 now
where the time goes in v1:
time: 104 us
  Pallas kernels  94.6 us (91%)
  local copies, waits for them, and re-layouts  8.66 us (8%)
    pallas_call x1, Pallas kernels, local(): pl.pallas_call(functools.partial(kernel, sizes), out_shape=(jax.ShapeDtyp...  94.6 us
    unnamed x19, local copies, waits for them, and re-layouts  8.66 us

profile of v1, /device:TPU:38, one launch (start us, length us, event | category | flops | bytes accessed | tf_op | source)
XLA Modules:
  0.0 103.9 jit_solution(1069462901869856250)
XLA Ops:
  0.6 0.0 copy-start.6
  0.6 0.0 copy-start.5
  0.7 0.7 copy-done.6
  1.3 0.0 copy-done.5
  1.3 0.0 copy-start
  1.3 1.0 copy-done
  2.3 0.0 copy-start.1
  2.4 1.0 copy-done.1
  3.4 0.0 copy-start.2
  3.4 1.0 copy-done.2
  4.4 0.0 copy-start.3
  4.4 0.7 copy-done.3
  5.1 0.0 copy-start.4
  5.1 0.7 copy-done.4
  5.8 94.6 %shard_map.110 = (bf16[8,896]{1,0:T(8,128)(2,1)S(1)}, bf16[8,896]{1,0:T(8,128)(2,1)S(1)}, bf16[896,256]{1,0:T(8,128)(2,1)S(1)}, bf16[896,256]{1,0:T(8,128)(2,1)S(1)}, bf16[256,896]{1,0:T(8,128)(2,1)S(1)}) custom-call(bf16[8,896]{1,0:T(8,128)(2,1)S(1)} %copy-done.3, bf16[8,896]{1,0:T(8,128)(2,1)S(1)} %copy-done.4, s32[2,8]{1,0:T(2,128)S(1)} %bitcast.2, ...), custom_call_target="tpu_custom_call" | custom-call | flops 1100000000 | bytes 3000000 | tf_op jit(solution)/shard_map/pallas_call | solution.py:289
  100.4 0.6 copy.17
  101.0 0.6 copy.18
  101.6 0.8 copy.19
  102.4 0.8 copy.20
  103.1 0.8 copy.21
Async XLA Ops:
  0.6 0.7 copy-start.6
  0.6 0.7 copy-start.5
  1.3 1.0 copy-start
  2.3 1.0 copy-start.1
  3.4 1.0 copy-start.2
  4.4 0.7 copy-start.3
  5.1 0.7 copy-start.4

commit v2 on v1

--- a/solution.py
+++ b/solution.py
@@ -14,15 +14,16 @@
 EXPERTS = 16
 UNIT = 16
 
-(DX, DG, GX, GG, SAB, SDH, AH, AD, RO, RX, BO, BX) = range(12)
+(DX, DG, GX, GG, SAB, SDH, AH, AD, RO, RX, BO, BX, UX, LX, UG, LG) = range(16)
 
 
 def iotas(shape):
     return lax.broadcasted_iota(I32, shape, 0), lax.broadcasted_iota(I32, shape, 1)
 
 
-def pick_table(rows, cols, routes, gates):
-    expert, token = rows >> 4, cols & 7
+def pick_table(rows, cols, mine, ne, routes, gates):
+    expert, token = (rows >> 4) + mine, cols & 7
+    expert = jnp.where(expert >= ne, expert - ne, expert)
     hot = jnp.zeros(rows.shape, F32)
     before = jnp.zeros(rows.shape, F32)
     gate = jnp.zeros(rows.shape, F32)
@@ -47,9 +48,10 @@
 
 def kernel(
     sizes,
-    tokens, cot, routes, gates, w_gate, w_up, w_down,
+    tokens_in, cot_in, routes_in, gates_in, w_gate, w_up, w_down,
     mixed, d_tokens, d_gate, d_up, d_down,
-    slot_x, slot_g, got_x, got_g, all_x, all_g, w_in, w_out,
+    tokens, cot, routes, gates,
+    slot_x, slot_g, got_x, got_g, via_x, via_g, all_x, all_g, w_in, w_out,
     part_ab, sum_ab, part_dh, sum_dh, hid, grads,
     out_s, out_r, dx_s, dx_r, back_os, back_or, back_xs, back_xr,
     grad_in, grad_out, spread,
@@ -65,16 +67,28 @@
     node, loc = lax.axis_index("node"), lax.axis_index("local")
     expert, shard = node // ns, node % ns
 
+    first = [
+        pltpu.make_async_copy(routes_in, routes, loads.at[6]),
+        pltpu.make_async_copy(gates_in, gates, loads.at[7]),
+        pltpu.make_async_copy(tokens_in, tokens, loads.at[8]),
+        pltpu.make_async_copy(cot_in, cot, loads.at[9]),
+    ]
     fetch = [
         pltpu.make_async_copy(w_gate, w_in.at[:, pl.ds(0, hidden_n)], loads.at[0]),
         pltpu.make_async_copy(w_up, w_in.at[:, pl.ds(hidden_n, hidden_n)], loads.at[1]),
         pltpu.make_async_copy(w_down, w_out, loads.at[2]),
     ]
-    for copy in fetch:
+    for copy in first + fetch:
         copy.start()
 
+    leg = ne // 4
+    up, low = ne // 2, (ne - 1) // 2
+    near = list(range(1, leg + 1)) + list(range(ne - leg, ne))
+
+    def at_expert(d):
+        return lax.rem(expert + d, ne) * ns + shard, loc
+
     far = sorted(range(1, ne), key=lambda d: -min(d, ne - d))
-    by_expert = [(lax.rem(expert + d, ne) * ns + shard, loc, lax.rem(expert + d, ne)) for d in far]
     by_shard = []
     for d in range(1, ns):
         other = lax.rem(shard + d, ns)
@@ -85,7 +99,7 @@
         by_local.append((node, other, other))
 
     barrier = pltpu.get_barrier_semaphore()
-    everyone = by_expert + by_shard + by_local
+    everyone = [(*at_expert(d), d) for d in near] + by_shard + by_local
     for to_node, to_loc, _ in everyone:
         pl.semaphore_signal(
             barrier, inc=1, device_id={"node": to_node, "local": to_loc}, device_id_type=MESH
@@ -115,8 +129,16 @@
     def rows(ref, index, n):
         return ref.at[pl.ds(pl.multiple_of(index * n, n), n)]
 
+    def units(ref, index, count=1):
+        return ref.at[pl.ds(index * UNIT, count * UNIT)]
+
+    def ship(phase, d, source, target):
+        push(phase, [(*at_expert(d), 0)], lambda _: source, lambda _: target)
+
+    for copy in first:
+        copy.wait()
     unit_rows = ne * UNIT
-    member, weighted = pick_table(*iotas((unit_rows, 64)), routes, gates)
+    member, weighted = pick_table(*iotas((unit_rows, 64)), expert, ne, routes, gates)
     pick = member.astype(BF)
     slot_gate = jnp.sum(weighted, axis=1, keepdims=True)
     tok = stacked(tokens[...].astype(F32), chunks).astype(BF)
@@ -125,11 +147,17 @@
     slot_g[...] = (jnp.dot(pick, grad_rows, preferred_element_type=F32) * slot_gate).astype(BF)
 
     pl.semaphore_wait(barrier, len(everyone))
-    push(DX, by_expert, lambda e: rows(slot_x, e, UNIT), lambda e: rows(got_x, expert, UNIT))
-    push(DG, by_expert, lambda e: rows(slot_g, e, UNIT), lambda e: rows(got_g, expert, UNIT))
-    own_unit = pl.ds(pl.multiple_of(expert * UNIT, UNIT), UNIT)
-    got_x[own_unit, :] = slot_x[own_unit, :]
-    got_g[own_unit, :] = slot_g[own_unit, :]
+    n_up, n_low = up - leg, low - leg
+    for slots, got, via, straight, above, below in (
+        (slot_x, got_x, via_x, DX, UX, LX),
+        (slot_g, got_g, via_g, DG, UG, LG),
+    ):
+        ship(above, leg, units(slots, leg + 1, n_up), units(via, 0, n_up))
+        if n_low:
+            ship(below, ne - leg, units(slots, up + 1, n_low), units(via, n_up, n_low))
+        for d in sorted(near, key=lambda d: -min(d, ne - d)):
+            ship(straight, d, units(slots, d), units(got, d))
+        got[0:UNIT, :] = slots[0:UNIT, :]
 
     a, b = iotas((chunks * per, unit_rows))
     q = lax.rem(a, per)
@@ -141,6 +169,14 @@
         flat = jnp.dot(spread[...], ref[...], preferred_element_type=F32).astype(BF)
         for j in range(chunks):
             target[own_rows, j * 128 : (j + 1) * 128] = flat[j * per : (j + 1) * per, :]
+
+    for got, via, straight, above, below in ((got_x, via_x, DX, UX, LX), (got_g, via_g, DG, UG, LG)):
+        arrived(above, via, n_up * UNIT)
+        for i in reversed(range(n_up)):
+            ship(straight, i + 1, units(via, i), units(got, leg + 1 + i))
+        arrived(below, via, n_low * UNIT)
+        for i in range(n_low):
+            ship(straight, ne - (n_low - i), units(via, n_up + i), units(got, up + 1 + i))
 
     arrived(DX, got_x, (ne - 1) * UNIT)
     unfold(got_x, all_x)
@@ -204,8 +240,9 @@
 
     arrived(RO, out_r, (ns - 1) * per)
     back_os[...] = fold(out_r)
-    push(BO, by_expert, lambda e: rows(back_os, e, UNIT), lambda e: rows(back_or, expert, UNIT))
-    back_or[own_unit, :] = back_os[own_unit, :]
+    for d in far:
+        ship(BO, ne - d, units(back_os, d), units(back_or, d))
+    back_or[0:UNIT, :] = back_os[0:UNIT, :]
 
     over_rows = (((0,), (0,)), ((), ()))
     grad_out[...] = lax.dot_general(
@@ -224,11 +261,12 @@
 
     arrived(RX, dx_r, (ns - 1) * per)
     back_xs[...] = fold(dx_r)
-    push(BX, by_expert, lambda e: rows(back_xs, e, UNIT), lambda e: rows(back_xr, expert, UNIT))
-    back_xr[own_unit, :] = back_xs[own_unit, :]
+    for d in far:
+        ship(BX, ne - d, units(back_xs, d), units(back_xr, d))
+    back_xr[0:UNIT, :] = back_xs[0:UNIT, :]
 
     cols, tall_rows = iotas((64, unit_rows))
-    member_t, weighted_t = pick_table(tall_rows, cols, routes, gates)
+    member_t, weighted_t = pick_table(tall_rows, cols, expert, ne, routes, gates)
     high = weighted_t.astype(BF)
     low = (weighted_t - high.astype(F32)).astype(BF)
 
@@ -244,8 +282,11 @@
     for j in range(chunks):
         d_tokens[:, j * 128 : (j + 1) * 128] = flat[j * 8 : (j + 1) * 8, :].astype(BF)
 
-    sent(DX, slot_x, (ne - 1) * UNIT)
-    sent(DG, slot_g, (ne - 1) * UNIT)
+    for phase in (DX, DG):
+        sent(phase, slot_x, (ne - 1) * UNIT)
+    for above, below in ((UX, LX), (UG, LG)):
+        sent(above, via_x, n_up * UNIT)
+        sent(below, via_x, n_low * UNIT)
     sent(GX, all_x, (ns - 1) * per)
     sent(GG, all_g, (ns - 1) * per)
     sent(SAB, part_ab, (nl - 1) * piece)
@@ -260,6 +301,16 @@
         copy.wait()
 
 
+def place(*refs):
+    count = len(refs) // 2
+    done = refs[-1]
+    copies = [pltpu.make_async_copy(refs[i], refs[count + i], done.at[i]) for i in range(count)]
+    for copy in copies:
+        copy.start()
+    for copy in copies:
+        copy.wait()
+
+
 def local(sizes, tokens, cotangent, routes, gates, w_gate, w_up, w_down):
     ne, ns, nl = sizes
     toks, width = tokens.shape
@@ -269,12 +320,14 @@
     chunks = width // 128
     unit_rows = ne * UNIT
     vmem = pl.BlockSpec(memory_space=pltpu.VMEM)
-    smem = pl.BlockSpec(memory_space=pltpu.SMEM)
     anywhere = pl.BlockSpec(memory_space=pl.ANY)
     unit = pltpu.VMEM((unit_rows, 128), BF)
     wide = pltpu.VMEM((rows_all, width), BF)
     scratch = (
-        [unit] * 4
+        [pltpu.VMEM(tokens.shape, BF)] * 2
+        + [pltpu.SMEM((2, toks), I32), pltpu.SMEM((2, toks), F32)]
+        + [unit] * 4
+        + [pltpu.VMEM((max(2, ne // 2 - 1) * UNIT, 128), BF)] * 2
         + [wide] * 2
         + [pltpu.VMEM((width, 2 * hidden_n), BF), pltpu.VMEM((hidden_n, width), BF)]
         + [pltpu.VMEM((rows_all, 2 * hidden_n), BF)] * 2
@@ -284,25 +337,33 @@
         + [unit] * 4
         + [pltpu.VMEM((width, 2 * hidden_n), BF), pltpu.VMEM((hidden_n, width), BF)]
         + [pltpu.VMEM((chunks * per, unit_rows), BF)]
-        + [pltpu.SemaphoreType.DMA((12,)), pltpu.SemaphoreType.DMA((12,)), pltpu.SemaphoreType.DMA((6,))]
+        + [pltpu.SemaphoreType.DMA((16,)), pltpu.SemaphoreType.DMA((16,)), pltpu.SemaphoreType.DMA((10,))]
     )
-    return pl.pallas_call(
-        functools.partial(kernel, sizes),
-        out_shape=(
+    shapes = (
             jax.ShapeDtypeStruct(tokens.shape, BF),
             jax.ShapeDtypeStruct(tokens.shape, BF),
             jax.ShapeDtypeStruct(w_gate.shape, BF),
             jax.ShapeDtypeStruct(w_up.shape, BF),
             jax.ShapeDtypeStruct(w_down.shape, BF),
-        ),
-        in_specs=[vmem, vmem, smem, smem, anywhere, anywhere, anywhere],
+    )
+    results = pl.pallas_call(
+        functools.partial(kernel, sizes),
+        out_shape=shapes,
+        in_specs=[anywhere] * 7,
         out_specs=(vmem, vmem, anywhere, anywhere, anywhere),
         scratch_shapes=scratch,
         compiler_params=pltpu.CompilerParams(
-            collective_id=0, has_side_effects=True, vmem_limit_bytes=32 * 1024 * 1024
+            collective_id=0, has_side_effects=True, vmem_limit_bytes=60 * 1024 * 1024
         ),
         cost_estimate=pl.CostEstimate(flops=1_100_000_000, bytes_accessed=3_000_000, transcendentals=8192),
     )(tokens, cotangent, routes.T, gates.T, w_gate, w_up, w_down)
+    return pl.pallas_call(
+        place,
+        out_shape=shapes,
+        in_specs=[anywhere] * 5,
+        out_specs=(anywhere,) * 5,
+        scratch_shapes=[pltpu.SemaphoreType.DMA((5,))],
+    )(*results)
 
 
 def build(mesh, experts):

time: 104 us -> 139 us (1.34)
  the two profiles are of different devices: /device:TPU:38 before, /device:TPU:6 now
where the time goes in v2:
time: 139 us; the launch traced here: 138 us
  Pallas kernels  137 us (99%)
    pallas_call x1, Pallas kernels, local(): pl.pallas_call(functools.partial(kernel, sizes), out_shape=shapes, in_spe...  93.4 us
    pallas_call x1, Pallas kernels, local(): pl.pallas_call(place, out_shape=shapes, in_specs=[anywhere] * 5, out_spec...  43.7 us

profile of v2, /device:TPU:6, one launch (start us, length us, event | category | flops | bytes accessed | tf_op | source)
XLA Modules:
  0.0 137.7 jit_solution(14634298878329390989)
XLA Ops:
  0.6 93.4 %shard_map.110 = (bf16[8,896]{1,0:T(8,128)(2,1)}, bf16[8,896]{1,0:T(8,128)(2,1)}, bf16[896,256]{1,0:T(8,128)(2,1)}, bf16[896,256]{1,0:T(8,128)(2,1)}, bf16[256,896]{1,0:T(8,128)(2,1)}) custom-call(bf16[8,896]{1,0:T(8,128)(2,1)} %tokens_in.1, bf16[8,896]{1,0:T(8,128)(2,1)} %cot_in.1, s32[2,8]{1,0:T(2,128)} %bitcast.2, f32[2,8]{1,0:T(2,128)} %bitcast.3, ...), custom_call_target="tpu_custom_call" | custom-call | flops 1100000000 | bytes 3000000 | tf_op jit(solution)/shard_map/pallas_call | solution.py:349
  94.0 43.7 %shard_map.111 = (bf16[8,896]{1,0:T(8,128)(2,1)}, bf16[8,896]{1,0:T(8,128)(2,1)}, bf16[896,256]{1,0:T(8,128)(2,1)}, bf16[896,256]{1,0:T(8,128)(2,1)}, bf16[256,896]{1,0:T(8,128)(2,1)}) custom-call(bf16[8,896]{1,0:T(8,128)(2,1)} %get-tuple-element.10.refs_0_, bf16[8,896]{1,0:T(8,128)(2,1)} %get-tuple-element.11.refs_1_, ...), custom_call_target="tpu_custom_call" | custom-call | tf_op jit(solution)/shard_map/pallas_call | solution.py:360

commit v3 on v2

v3 whole, which is shorter than its diff:
```python
import functools

import jax
import jax.numpy as jnp
from jax import lax
from jax.experimental import pallas as pl
from jax.experimental.pallas import tpu as pltpu
from jax.sharding import PartitionSpec as P

MESH = pl.DeviceIdType.MESH
BF = jnp.bfloat16
F32 = jnp.float32
I32 = jnp.int32
EXPERTS = 16
UNIT = 16

(DX, DG, GX, GG, SAB, SDH, AH, AD, RO, RX, BO, BX) = range(0, 24, 2)
(UX, LX, UG, LG) = range(24, 28)
PHASES = 28


def iotas(shape):
    return lax.broadcasted_iota(I32, shape, 0), lax.broadcasted_iota(I32, shape, 1)


def pick_table(rows, cols, mine, ne, routes, gates):
    expert, token = (rows >> 4) + mine - ne // 4, cols & 7
    expert = jnp.where(expert >= ne, expert - ne, jnp.where(expert < 0, expert + ne, expert))
    hot = jnp.zeros(rows.shape, F32)
    before = jnp.zeros(rows.shape, F32)
    gate = jnp.zeros(rows.shape, F32)
    for t in range(8):
        first, second = expert == routes[0, t], expert == routes[1, t]
        here = token == t
        named = jnp.where(first | second, 1.0, 0.0)
        hot = hot + jnp.where(here, named, 0.0)
        before = before + jnp.where(token > t, named, 0.0)
        weight = jnp.where(first, gates[0, t], 0.0) + jnp.where(second, gates[1, t], 0.0)
        gate = gate + jnp.where(here, weight, 0.0)
    slot = (rows & 1).astype(F32)
    keep = (((rows & 15) >> 1) == (cols >> 3)) & (before == slot)
    return jnp.where(keep, hot, 0.0), jnp.where(keep, gate, 0.0)


def stacked(value, chunks):
    parts = [value[:, j * 128 : (j + 1) * 128] for j in range(chunks)]
    parts = parts + [jnp.zeros_like(parts[0])] * (8 - chunks)
    return jnp.concatenate(parts, axis=0)


def kernel(
    sizes,
    tokens_in, cot_in, routes_in, gates_in, w_gate, w_up, w_down,
    mixed, d_tokens, d_gate, d_up, d_down,
    tokens, cot, routes, gates,
    slot_x, slot_g, got_x, got_g, via_x, via_g, all_x, all_g, w_in, w_out,
    part_ab, sum_ab, part_dh, sum_dh, hid, grads,
    out_s, out_r, dx_s, dx_r, back_os, back_or, back_xs, back_xr,
    grad_in, grad_out, spread,
    send, recv, loads,
):
    ne, ns, nl = sizes
    width = tokens.shape[1]
    chunks = width // 128
    hidden_n = w_gate.shape[1]
    quarter = ne // 4
    per = ne
    half = per * ns
    piece = half // nl
    half_units = ne // 2
    unit_rows = ne * UNIT
    node, loc = lax.axis_index("node"), lax.axis_index("local")
    expert, shard = node // ns, node % ns

    first = [
        pltpu.make_async_copy(routes_in, routes, loads.at[6]),
        pltpu.make_async_copy(gates_in, gates, loads.at[7]),
        pltpu.make_async_copy(tokens_in, tokens, loads.at[8]),
        pltpu.make_async_copy(cot_in, cot, loads.at[9]),
    ]
    fetch = [
        pltpu.make_async_copy(w_gate, w_in.at[:, pl.ds(0, hidden_n)], loads.at[0]),
        pltpu.make_async_copy(w_up, w_in.at[:, pl.ds(hidden_n, hidden_n)], loads.at[1]),
        pltpu.make_async_copy(w_down, w_out, loads.at[2]),
    ]
    for copy in first + fetch:
        copy.start()

    def at_expert(d):
        return lax.rem(expert + d % ne, ne) * ns + shard, loc

    near = [d for d in range(-quarter, quarter + 1) if d]
    by_shard = []
    for d in range(1, ns):
        other = lax.rem(shard + d, ns)
        by_shard.append((expert * ns + other, loc, other))
    by_local = []
    for d in range(1, nl):
        other = lax.rem(loc + d, nl)
        by_local.append((node, other, other))

    barrier = pltpu.get_barrier_semaphore()
    everyone = [(*at_expert(d), d) for d in near] + by_shard + by_local
    for to_node, to_loc, _ in everyone:
        pl.semaphore_signal(
            barrier, inc=1, device_id={"node": to_node, "local": to_loc}, device_id_type=MESH
        )

    def push(phase, peers, source, target):
        for to_node, to_loc, index in peers:
            pltpu.make_async_remote_copy(
                src_ref=source(index),
                dst_ref=target(index),
                send_sem=send.at[phase],
                recv_sem=recv.at[phase],
                device_id={"node": to_node, "local": to_loc},
                device_id_type=MESH,
            ).start()

    def arrived(phase, ref, count):
        if count > 0:
            part = ref.at[pl.ds(0, count)]
            pltpu.make_async_copy(part, part, recv.at[phase]).wait()

    def sent(phase, ref, count):
        if count > 0:
            part = ref.at[pl.ds(0, count)]
            pltpu.make_async_copy(part, part, send.at[phase]).wait()

    def span(h, index, n):
        return pl.ds(pl.multiple_of(h * half + index * n, n), n)

    def units(ref, index, count=1):
        return ref.at[pl.ds(index * UNIT, count * UNIT)]

    def spot(d):
        return (d + quarter) % ne

    def ship(phase, d, source, target):
        push(phase, [(*at_expert(d), 0)], lambda _: source, lambda _: target)

    for copy in first:
        copy.wait()
    member, weighted = pick_table(*iotas((unit_rows, 64)), expert, ne, routes, gates)
    pick = member.astype(BF)
    slot_gate = jnp.sum(weighted, axis=1, keepdims=True)
    tok = stacked(tokens[...].astype(F32), chunks).astype(BF)
    slot_x[...] = jnp.dot(pick, tok, preferred_element_type=F32).astype(BF)
    grad_rows = stacked(cot[...].astype(F32), chunks).astype(BF)
    slot_g[...] = (jnp.dot(pick, grad_rows, preferred_element_type=F32) * slot_gate).astype(BF)

    pl.semaphore_wait(barrier, len(everyone))
    n_up, n_low = quarter, quarter - 1
    up_at, low_at = spot(quarter + 1), spot(2 * quarter + 1)
    kinds = ((slot_x, got_x, via_x, DX, UX, LX), (slot_g, got_g, via_g, DG, UG, LG))
    for slots, got, via, straight, above, below in kinds:
        ship(above, quarter, units(slots, up_at, n_up), units(via, 0, n_up))
        if n_low:
            ship(below, -quarter, units(slots, low_at, n_low), units(via, n_up, n_low))
        ship(straight + 1, quarter, units(slots, spot(quarter)), units(got, spot(quarter)))
    for slots, got, via, straight, above, below in kinds:
        for d in sorted(near, key=lambda d: -abs(d)):
            if d != quarter:
                ship(straight, d, units(slots, spot(d)), units(got, spot(d)))
        own = spot(0) * UNIT
        got[own : own + UNIT, :] = slots[own : own + UNIT, :]

    a, b = iotas((chunks * per, half_units * UNIT))
    q = lax.rem(a, per)
    spread[...] = jnp.where(b == (q >> 1) * UNIT + 2 * (a // per) + (q & 1), 1.0, 0.0).astype(BF)

    for slots, got, via, straight, above, below in kinds:
        arrived(above, via, n_up * UNIT)
        for i in reversed(range(n_up)):
            ship(straight + 1, i + 1, units(via, i), units(got, up_at + i))
        arrived(below, via, n_low * UNIT)
        for i in range(n_low):
            ship(straight + 1, i - n_low, units(via, n_up + i), units(got, low_at + i))

    def gather(h, phase_in, phase_out, ref, target):
        arrived(phase_in + h, ref, (half_units - 1 + h) * UNIT)
        rows = ref[h * half_units * UNIT : (h + 1) * half_units * UNIT, :]
        flat = jnp.dot(spread[...], rows, preferred_element_type=F32).astype(BF)
        own_rows = span(h, shard, per)
        for j in range(chunks):
            target[own_rows, j * 128 : (j + 1) * 128] = flat[j * per : (j + 1) * per, :]
        push(phase_out + h, by_shard, lambda s: target.at[own_rows], lambda s: target.at[own_rows])

    def block(h):
        return slice(h * half, (h + 1) * half)

    def scatter(h, phase, part, where, peers, n, me):
        push(phase + h, peers, lambda i: part.at[span(h, i, n)], lambda i: where.at[span(h, me, n)])
        where[span(h, me, n), :] = part[span(h, me, n), :]

    def products(h):
        arrived(GX + h, all_x, (ns - 1) * per)
        part_ab[block(h), :] = jnp.dot(all_x[block(h), :], w_in[...], preferred_element_type=F32).astype(BF)
        scatter(h, SAB, part_ab, sum_ab, by_local, piece, loc)

    def hidden_grads(h):
        arrived(GG + h, all_g, (ns - 1) * per)
        part_dh[block(h), :] = lax.dot_general(
            all_g[block(h), :], w_out[...], (((1,), (1,)), ((), ())), preferred_element_type=F32
        ).astype(BF)
        scatter(h, SDH, part_dh, sum_dh, by_local, piece, loc)

    def total(ref, h, n, count):
        base = h * half
        value = ref[base : base + n, :].astype(F32)
        for i in range(1, count):
            value = value + ref[base + i * n : base + (i + 1) * n, :].astype(F32)
        return value

    def spread_local(h, phase, ref):
        mine = span(h, loc, piece)
        push(phase + h, by_local, lambda l: ref.at[mine], lambda l: ref.at[mine])

    kept = {}

    def activate(h):
        arrived(SAB + h, sum_ab, (nl - 1) * piece)
        ab = total(sum_ab, h, piece, nl)
        a_val, b_val = ab[:, :hidden_n], ab[:, hidden_n:]
        sig = jax.nn.sigmoid(a_val)
        kept[h] = (a_val, b_val, sig)
        hid[span(h, loc, piece), :] = (a_val * sig * b_val).astype(BF)
        spread_local(h, AH, hid)

    def differentiate(h):
        a_val, b_val, sig = kept[h]
        arrived(SDH + h, sum_dh, (nl - 1) * piece)
        dh = total(sum_dh, h, piece, nl)
        mine = span(h, loc, piece)
        grads[mine, 0:hidden_n] = (dh * b_val * sig * (1.0 + a_val * (1.0 - sig))).astype(BF)
        grads[mine, hidden_n : 2 * hidden_n] = (dh * a_val * sig).astype(BF)
        spread_local(h, AD, grads)

    def outputs(h):
        arrived(AH + h, hid, (nl - 1) * piece)
        out_s[block(h), :] = jnp.dot(hid[block(h), :], w_out[...], preferred_element_type=F32).astype(BF)
        scatter(h, RO, out_s, out_r, by_shard, per, shard)

    def input_grads(h):
        arrived(AD + h, grads, (nl - 1) * piece)
        dx_s[block(h), :] = lax.dot_general(
            grads[block(h), :], w_in[...], (((1,), (1,)), ((), ())), preferred_element_type=F32
        ).astype(BF)
        scatter(h, RX, dx_s, dx_r, by_shard, per, shard)

    def give_back(h, phase_in, phase_out, ref, source, target):
        arrived(phase_in + h, ref, (ns - 1) * per)
        value = total(ref, h, per, ns).astype(BF)
        tall = jnp.concatenate([value[:, j * 128 : (j + 1) * 128] for j in range(chunks)], axis=0)
        at = h * half_units * UNIT
        source[at : at + half_units * UNIT, :] = lax.dot_general(
            spread[...], tall, (((0,), (0,)), ((), ())), preferred_element_type=F32
        ).astype(BF)
        wanted = [d for d in range(-2 * quarter + 1, 2 * quarter + 1) if d and spot(d) // half_units == h]
        for d in sorted(wanted, key=lambda d: -abs(d)):
            ship(phase_out + h, -d, units(source, spot(d)), units(target, spot(d)))
        if h == 0:
            own = spot(0) * UNIT
            target[own : own + UNIT, :] = source[own : own + UNIT, :]

    gather(0, DX, GX, got_x, all_x)
    gather(0, DG, GG, got_g, all_g)
    for copy in fetch:
        copy.wait()
    gather(1, DX, GX, got_x, all_x)
    products(0)
    gather(1, DG, GG, got_g, all_g)
    hidden_grads(0)
    products(1)
    activate(0)
    hidden_grads(1)
    differentiate(0)
    activate(1)
    outputs(0)
    differentiate(1)
    input_grads(0)
    outputs(1)
    input_grads(1)
    give_back(0, RO, BO, out_r, back_os, back_or)
    give_back(0, RX, BX, dx_r, back_xs, back_xr)
    give_back(1, RO, BO, out_r, back_os, back_or)
    give_back(1, RX, BX, dx_r, back_xs, back_xr)

    over_rows = (((0,), (0,)), ((), ()))
    grad_out[...] = lax.dot_general(
        hid[...], all_g[...], over_rows, preferred_element_type=F32
    ).astype(BF)
    grad_in[...] = lax.dot_general(
        all_x[...], grads[...], over_rows, preferred_element_type=F32
    ).astype(BF)
    store = [
        pltpu.make_async_copy(grad_in.at[:, pl.ds(0, hidden_n)], d_gate, loads.at[3]),
        pltpu.make_async_copy(grad_in.at[:, pl.ds(hidden_n, hidden_n)], d_up, loads.at[4]),
        pltpu.make_async_copy(grad_out, d_down, loads.at[5]),
    ]
    for copy in store:
        copy.start()

    cols, tall_rows = iotas((64, unit_rows))
    member_t, weighted_t = pick_table(tall_rows, cols, expert, ne, routes, gates)
    high = weighted_t.astype(BF)
    low = (weighted_t - high.astype(F32)).astype(BF)

    for h in range(2):
        arrived(BO + h, back_or, (half_units - 1 + h) * UNIT)
    value = back_or[...]
    flat = jnp.dot(high, value, preferred_element_type=F32) + jnp.dot(
        low, value, preferred_element_type=F32
    )
    for j in range(chunks):
        mixed[:, j * 128 : (j + 1) * 128] = flat[j * 8 : (j + 1) * 8, :].astype(BF)
    for h in range(2):
        arrived(BX + h, back_xr, (half_units - 1 + h) * UNIT)
    flat = jnp.dot(member_t.astype(BF), back_xr[...], preferred_element_type=F32)
    for j in range(chunks):
        d_tokens[:, j * 128 : (j + 1) * 128] = flat[j * 8 : (j + 1) * 8, :].astype(BF)

    for above, below in ((UX, LX), (UG, LG)):
        sent(above, via_x, n_up * UNIT)
        sent(below, via_x, n_low * UNIT)
    for h in range(2):
        for phase in (DX, DG, BO, BX):
            sent(phase + h, slot_x, (half_units - 1 + h) * UNIT)
        for phase, ref in ((GX, all_x), (GG, all_g), (RO, out_s), (RX, dx_s)):
            sent(phase + h, ref, (ns - 1) * per)
        for phase, ref in ((SAB, part_ab), (SDH, part_dh), (AH, hid), (AD, grads)):
            sent(phase + h, ref, (nl - 1) * piece)
    for copy in store:
        copy.wait()


def place(*refs):
    count = len(refs) // 3
    source, target, held, done = refs[:count], refs[count : 2 * count], refs[2 * count : -1], refs[-1]
    reads = [pltpu.make_async_copy(source[i], held[i], done.at[i]) for i in range(count)]
    writes = [pltpu.make_async_copy(held[i], target[i], done.at[count + i]) for i in range(count)]
    for copy in reads:
        copy.start()
    for read, write in zip(reads, writes):
        read.wait()
        write.start()
    for copy in writes:
        copy.wait()


def local(sizes, tokens, cotangent, routes, gates, w_gate, w_up, w_down):
    ne, ns, nl = sizes
    toks, width = tokens.shape
    hidden_n = w_gate.shape[1]
    per = ne * 2
    rows_all = per * ns
    chunks = width // 128
    unit_rows = ne * UNIT
    vmem = pl.BlockSpec(memory_space=pltpu.VMEM)
    anywhere = pl.BlockSpec(memory_space=pl.ANY)
    unit = pltpu.VMEM((unit_rows, 128), BF)
    wide = pltpu.VMEM((rows_all, width), BF)
    scratch = (
        [pltpu.VMEM(tokens.shape, BF)] * 2
        + [pltpu.SMEM((2, toks), I32), pltpu.SMEM((2, toks), F32)]
        + [unit] * 4
        + [pltpu.VMEM((max(2, ne // 2 - 1) * UNIT, 128), BF)] * 2
        + [wide] * 2
        + [pltpu.VMEM((width, 2 * hidden_n), BF), pltpu.VMEM((hidden_n, width), BF)]
        + [pltpu.VMEM((rows_all, 2 * hidden_n), BF)] * 2
        + [pltpu.VMEM((rows_all, hidden_n), BF)] * 2
        + [pltpu.VMEM((rows_all, hidden_n), BF), pltpu.VMEM((rows_all, 2 * hidden_n), BF)]
        + [wide] * 4
        + [unit] * 4
        + [pltpu.VMEM((width, 2 * hidden_n), BF), pltpu.VMEM((hidden_n, width), BF)]
        + [pltpu.VMEM((chunks * ne, unit_rows // 2), BF)]
        + [pltpu.SemaphoreType.DMA((PHASES,)), pltpu.SemaphoreType.DMA((PHASES,)), pltpu.SemaphoreType.DMA((10,))]
    )
    shapes = (
            jax.ShapeDtypeStruct(tokens.shape, BF),
            jax.ShapeDtypeStruct(tokens.shape, BF),
            jax.ShapeDtypeStruct(w_gate.shape, BF),
            jax.ShapeDtypeStruct(w_up.shape, BF),
            jax.ShapeDtypeStruct(w_down.shape, BF),
    )
    results = pl.pallas_call(
        functools.partial(kernel, sizes),
        out_shape=shapes,
        in_specs=[anywhere] * 7,
        out_specs=(vmem, vmem, anywhere, anywhere, anywhere),
        scratch_shapes=scratch,
        compiler_params=pltpu.CompilerParams(
            collective_id=0, has_side_effects=True, vmem_limit_bytes=60 * 1024 * 1024
        ),
        cost_estimate=pl.CostEstimate(flops=1_100_000_000, bytes_accessed=3_000_000, transcendentals=8192),
    )(tokens, cotangent, routes.T, gates.T, w_gate, w_up, w_down)
    return pl.pallas_call(
        place,
        out_shape=shapes,
        in_specs=[anywhere] * 5,
        out_specs=(anywhere,) * 5,
        scratch_shapes=[pltpu.VMEM(r.shape, BF) for r in results] + [pltpu.SemaphoreType.DMA((10,))],
    )(*results)


def build(mesh, experts):
    shards = mesh.shape["node"] // experts
    sizes = (experts, shards, mesh.shape["local"])
    return jax.shard_map(
        functools.partial(local, sizes),
        mesh=mesh,
        in_specs=(
            P("node", "local"),
            P("node", "local"),
            P("node", None),
            P("node", None),
            P("local", "node"),
            P("local", "node"),
            P("node", "local"),
        ),
        out_specs=(
            P("node", "local"),
            P("node", "local"),
            P("local", "node"),
            P("local", "node"),
            P("node", "local"),
        ),
        check_vma=False,
    )


def solution(mesh):
    return build(mesh, EXPERTS)
```

time: 139 us -> 92.1 us (0.66)
  Pallas kernels: 137 us -> 91.2 us
    pallas_call x1, Pallas kernels: 43.7 us -> 2.21 us  [local(): pl.pallas_call(place, out_shape=shapes, in_specs=[anywhere] * 5, out_spec...]
    pallas_call x1, Pallas kernels: 93.4 us -> 89 us  [local(): pl.pallas_call(functools.partial(kernel, sizes), out_shape=shapes, in_spe...]
where the time goes in v3:
time: 92.1 us; the launch traced here: 91.9 us
  Pallas kernels  91.2 us (99%)
    pallas_call x1, Pallas kernels, local(): pl.pallas_call(functools.partial(kernel, sizes), out_shape=shapes, in_spe...  89 us
    pallas_call x1, Pallas kernels, local(): pl.pallas_call(place, out_shape=shapes, in_specs=[anywhere] * 5, out_spec...  2.21 us

profile of v3, /device:TPU:6, one launch (start us, length us, event | category | flops | bytes accessed | tf_op | source)
XLA Modules:
  0.0 91.9 jit_solution(4200026552381893842)
XLA Ops:
  0.6 89.0 %shard_map.110 = (bf16[8,896]{1,0:T(8,128)(2,1)}, bf16[8,896]{1,0:T(8,128)(2,1)}, bf16[896,256]{1,0:T(8,128)(2,1)}, bf16[896,256]{1,0:T(8,128)(2,1)}, bf16[256,896]{1,0:T(8,128)(2,1)}) custom-call(bf16[8,896]{1,0:T(8,128)(2,1)} %tokens_in.1, bf16[8,896]{1,0:T(8,128)(2,1)} %cot_in.1, s32[2,8]{1,0:T(2,128)} %bitcast.2, f32[2,8]{1,0:T(2,128)} %bitcast.3, ...), custom_call_target="tpu_custom_call" | custom-call | flops 1100000000 | bytes 3000000 | tf_op jit(solution)/shard_map/pallas_call | solution.py:386
  89.6 2.2 %shard_map.111 = (bf16[8,896]{1,0:T(8,128)(2,1)}, bf16[8,896]{1,0:T(8,128)(2,1)}, bf16[896,256]{1,0:T(8,128)(2,1)}, bf16[896,256]{1,0:T(8,128)(2,1)}, bf16[256,896]{1,0:T(8,128)(2,1)}) custom-call(bf16[8,896]{1,0:T(8,128)(2,1)} %get-tuple-element.10.refs_0_, bf16[8,896]{1,0:T(8,128)(2,1)} %get-tuple-element.11.refs_1_, ...), custom_call_target="tpu_custom_call" | custom-call | tf_op jit(solution)/shard_map/pallas_call | solution.py:397

commit v4 on v3

--- a/solution.py
+++ b/solution.py
@@ -91,11 +91,11 @@
 
     near = [d for d in range(-quarter, quarter + 1) if d]
     by_shard = []
-    for d in range(1, ns):
+    for d in sorted(range(1, ns), key=lambda d: -min(d % 4, 4 - d % 4)):
         other = lax.rem(shard + d, ns)
         by_shard.append((expert * ns + other, loc, other))
     by_local = []
-    for d in range(1, nl):
+    for d in sorted(range(1, nl), key=lambda d: -min(d, nl - d)):
         other = lax.rem(loc + d, nl)
         by_local.append((node, other, other))
 
@@ -271,19 +271,19 @@
     products(0)
     gather(1, DG, GG, got_g, all_g)
     hidden_grads(0)
+    activate(0)
     products(1)
-    activate(0)
     hidden_grads(1)
+    activate(1)
     differentiate(0)
-    activate(1)
     outputs(0)
+    outputs(1)
     differentiate(1)
     input_grads(0)
-    outputs(1)
     input_grads(1)
     give_back(0, RO, BO, out_r, back_os, back_or)
+    give_back(1, RO, BO, out_r, back_os, back_or)
     give_back(0, RX, BX, dx_r, back_xs, back_xr)
-    give_back(1, RO, BO, out_r, back_os, back_or)
     give_back(1, RX, BX, dx_r, back_xs, back_xr)
 
     over_rows = (((0,), (0,)), ((), ()))

time: 92.1 us -> 89.6 us (0.973)
  Pallas kernels: 91.2 us -> 88.7 us
    pallas_call x1, Pallas kernels: 89 us -> 86.4 us  [local(): pl.pallas_call(functools.partial(kernel, sizes), out_shape=shapes, in_spe...]
where the time goes in v4:
time: 89.6 us; the launch traced here: 89.3 us
  Pallas kernels  88.7 us (99%)
    pallas_call x1, Pallas kernels, local(): pl.pallas_call(functools.partial(kernel, sizes), out_shape=shapes, in_spe...  86.4 us
    pallas_call x1, Pallas kernels, local(): pl.pallas_call(place, out_shape=shapes, in_specs=[anywhere] * 5, out_spec...  2.21 us

profile of v4, /device:TPU:6, one launch (start us, length us, event | category | flops | bytes accessed | tf_op | source)
XLA Modules:
  0.0 89.3 jit_solution(12896879122506562623)
XLA Ops:
  0.6 86.4 %shard_map.110 = (bf16[8,896]{1,0:T(8,128)(2,1)}, bf16[8,896]{1,0:T(8,128)(2,1)}, bf16[896,256]{1,0:T(8,128)(2,1)}, bf16[896,256]{1,0:T(8,128)(2,1)}, bf16[256,896]{1,0:T(8,128)(2,1)}) custom-call(bf16[8,896]{1,0:T(8,128)(2,1)} %tokens_in.1, bf16[8,896]{1,0:T(8,128)(2,1)} %cot_in.1, s32[2,8]{1,0:T(2,128)} %bitcast.2, f32[2,8]{1,0:T(2,128)} %bitcast.3, ...), custom_call_target="tpu_custom_call" | custom-call | flops 1100000000 | bytes 3000000 | tf_op jit(solution)/shard_map/pallas_call | solution.py:386
  87.1 2.2 %shard_map.111 = (bf16[8,896]{1,0:T(8,128)(2,1)}, bf16[8,896]{1,0:T(8,128)(2,1)}, bf16[896,256]{1,0:T(8,128)(2,1)}, bf16[896,256]{1,0:T(8,128)(2,1)}, bf16[256,896]{1,0:T(8,128)(2,1)}) custom-call(bf16[8,896]{1,0:T(8,128)(2,1)} %get-tuple-element.10.refs_0_, bf16[8,896]{1,0:T(8,128)(2,1)} %get-tuple-element.11.refs_1_, ...), custom_call_target="tpu_custom_call" | custom-call | tf_op jit(solution)/shard_map/pallas_call | solution.py:397
